TPU v7x, 512 devices: a whole 4x4x16 slice. The times are simulated.
512 devices in a mesh: gx: 4 (over z_lo), gy: 8 (over x, core), gz: 16 (over y, z_hi).
Axes of the slice: x: 4, y: 4, z: 16 (z_hi: 4, z_lo: 4; z = z_hi * 4 + z_lo), core: 2. Of those that a mesh axis runs over, the one named last changes fastest.
Arguments:
- final_adjoint: float32 [9, 56, 65536], P(None, None, ('gx', 'gy', 'gz')), may hold values from -6 to 6
- star_mats: float32 [3, 9, 9, 65536], P(None, None, None, ('gx', 'gy', 'gz')), may hold values from -6 to 6
- deriv_stiff: float32 [3, 56, 56], replicated, may hold values from -6 to 6
- volume_stiffness: float32 [3, 56, 56], replicated, may hold values from -0.21875 to 0.21875
- face_projection: float32 [4, 21, 56], replicated, may hold values from -0.75 to 0.75
- flux_local: float32 [4, 9, 9, 65536], P(None, None, None, ('gx', 'gy', 'gz')), may hold values from -0.875 to 0.875
- flux_across: float32 [4, 9, 9, 65536], P(None, None, None, ('gx', 'gy', 'gz')), may hold values from -0.875 to 0.875
- cluster: int32 [65536], P(('gx', 'gy', 'gz')), may hold values from 0 to 1, as said below
- partner: int32 [4, 65536], P(None, ('gx', 'gy', 'gz')), may hold values from 0 to 703, as said below
- send_slots: int32 [6, 16384], P(None, ('gx', 'gy', 'gz')), may hold values from 0 to 511, as said below
Outputs:
- initial_adjoint: float32 [9, 56, 65536], P(None, None, ('gx', 'gy', 'gz'))
Inputs may be any that keep to these rules, and one draw needn't show every extreme that they name: At most 64 of a partition's elements have cluster 0, some partition has exactly 64, and every partition has at least three sixteenths of 128. `send_slots`: row d of a partition lists 32 distinct face slots c * 128 + e lying on its boundary toward direction d; no slot is in two rows. At most 16 slots of a row belong to cluster-0 elements, and some row of some partition has exactly 16. partner[c, e] = 512 + d * 32 + j exactly when send_slots[d, j] of the partition is c * 128 + e; every other slot's partner is another slot of the same partition below 512 whose partner is it.
All inputs are finite; a program needn't handle non-finite values.
Results may differ from a plain program's by a relative error of at most 0.0003.
Values sent between devices are 32-bit elements; how exact they have to be, the bound alone decides.
A program may use at most 64 MiB of HBM per device.

v0:
```python
import math

import jax
import jax.numpy as jnp
from jax import lax
from jax.experimental import pallas as pl
from jax.experimental.pallas import tpu as pltpu
from jax.sharding import PartitionSpec as P

MESH = pl.DeviceIdType.MESH
TERMS = 6
STEPS = 4
FINE = 1.0 / STEPS
NF = 9
NM = 56
NB = 21
PB = 24
LN = 128
F32 = jnp.float32
B16 = jnp.bfloat16


def coefficients(lower, upper):
    return [(upper ** (k + 1) - lower ** (k + 1)) / math.factorial(k + 1) for k in range(TERMS)]


FAST = coefficients(0.0, FINE)
WHOLE = coefficients(0.0, 1.0)
SLOW = [coefficients(s * FINE, (s + 1) * FINE) for s in range(STEPS)]


def two(x):
    high = x.astype(B16)
    return high, (x - high.astype(F32)).astype(B16)


def nn(a, b):
    return jnp.dot(a, b, preferred_element_type=F32)


def nt(a, b):
    return lax.dot_general(a, b, (((1,), (1,)), ((), ())), preferred_element_type=F32)


def stack3(x):
    high, low = two(x)
    return jnp.concatenate([high, low, high], axis=0)


def left3(x):
    high, low = two(x)
    return jnp.concatenate([high, high, low], axis=1)


def rows64(x):
    return jnp.concatenate([x, jnp.zeros((64 - NM, LN), F32)], axis=0)


def iota(shape, dim):
    return lax.broadcasted_iota(jnp.int32, shape, dim).astype(F32)


def hot(mask):
    return jnp.where(mask, 1.0, 0.0)


def pick(a, cm2):
    high, low = two(a)
    return nt(high, cm2) + nt(low, cm2)


def kernel(
    y_ref, star_ref, ds_ref, vs_ref, fp_ref, fl_ref, fa_ref, cl_ref, pa_ref, ss_ref, o_ref,
    A3, V3, P3, PT3, PF, AF, X9, Xp, T9, Tp, TR9, TRp, SF, SS, CE, CO, STARF, FLF, FAF, Yp, Sp, SB, MF, Z9, Zp, TOT,
    send3, recv3, send, recv, ssem3, rsem3, ssem, rsem,
):
    place = [lax.axis_index(a) for a in ("gx", "gy", "gz")]
    sizes = [lax.axis_size(a) for a in ("gx", "gy", "gz")]
    sides = []
    for d in range(6):
        axis, up = d // 2, d % 2
        there = place[axis] < sizes[axis] - 1 if up else place[axis] > 0
        target = list(place)
        target[axis] = place[axis] + (1 if up else -1)
        sides.append((there, tuple(target)))
    peers = sum(there.astype(jnp.int32) for there, _ in sides)

    barrier = pltpu.get_barrier_semaphore()
    for there, target in sides:
        @pl.when(there)
        def _():
            pl.semaphore_signal(barrier, inc=1, device_id=target, device_id_type=MESH)

    def link(s, d, arriving):
        to = d if arriving else d ^ 1
        target = sides[d][1]
        if s == STEPS - 1:
            pairs = [(send3.at[h, d], recv3.at[h, to], ssem3.at[h, d], rsem3.at[h, to]) for h in range(2)]
        else:
            pairs = [(send.at[s, d], recv.at[s, to], ssem.at[s, d], rsem.at[s, to])]
        return [
            pltpu.make_async_remote_copy(
                src_ref=a, dst_ref=b, send_sem=c, recv_sem=e, device_id=target, device_id_type=MESH)
            for a, b, c, e in pairs
        ]

    def start_all(s):
        for d in range(6):
            @pl.when(sides[d][0])
            def _():
                for copy in link(s, d, False):
                    copy.start()

    def arrive_all(s):
        for d in range(6):
            @pl.when(sides[d][0])
            def _():
                for copy in link(s, d, True):
                    copy.wait_recv()

    def sent_all(s):
        for d in range(6):
            @pl.when(sides[d][0])
            def _():
                for copy in link(s, d, False):
                    copy.wait_send()

    low_half = lax.broadcasted_iota(jnp.int32, (1, LN), 1) < 64

    PF[...] = jnp.zeros((96, LN), F32)
    for c in range(4):
        PF[c * PB : c * PB + NB, 0:NM] = fp_ref[c]
    pf = PF[...]
    P3[...] = left3(pf[:, 0:64])
    SF[...] = jnp.zeros(SF.shape, F32)
    for d in range(6):
        there, _ = sides[d]

        @pl.when(jnp.logical_not(there))
        def _():
            for half in range(2):
                recv3[half, d] = jnp.zeros((16, 256), F32)
            for s in range(STEPS - 1):
                recv[s, d] = jnp.zeros((16, 256), F32)

    for f in range(NF):
        X9[:, f * LN : (f + 1) * LN] = stack3(rows64(y_ref[f]))
    TR9[...] = nn(P3[...], X9[...])

    def flux_full(ref, emit):
        for c in range(4):
            acc = [None] * NF
            for f in range(NF):
                t = TR9[c * PB : (c + 1) * PB, f * LN : (f + 1) * LN]
                for g in range(NF):
                    p = ref[c, g, f : f + 1, :] * t
                    acc[g] = p if acc[g] is None else acc[g] + p
            for g in range(NF):
                emit(c, g, acc[g])

    def put_sent(c, g, value):
        SF[g * PB : (g + 1) * PB, c * LN : (c + 1) * LN] = value

    flux_full(fa_ref, put_sent)

    fast = hot(cl_ref[...] == 0)
    fast512 = jnp.concatenate([fast] * 4, axis=1)
    slow512 = 1.0 - fast512
    eye = iota((32, 32), 0) == iota((32, 32), 1)
    lane512 = iota((32, 512), 1)
    parts = []
    for d in range(6):
        row = ss_ref[d : d + 1, :].astype(F32)
        column = jnp.sum(jnp.where(eye, row, 0.0), axis=1, keepdims=True)
        parts.append(hot(lane512 == column))
    slots = jnp.concatenate(parts, axis=0).astype(B16)
    flags = nt(jnp.broadcast_to(fast512, (16, 512)).astype(B16), slots)
    i_sub, i_lane = lax.broadcasted_iota(jnp.int32, (192, 192), 0), lax.broadcasted_iota(jnp.int32, (192, 192), 1)
    earlier = hot(jnp.logical_and(i_sub // 32 == i_lane // 32, i_sub < i_lane)).astype(B16)
    ranks = nn(flags.astype(B16), earlier)[0:1, :]
    flags = flags[0:1, :]
    lane192 = lax.broadcasted_iota(jnp.int32, (1, 192), 1)
    j_row = (lane192 % 32).astype(F32)
    position = jnp.where(flags > 0.5, ranks, 31.0 - (j_row - ranks))
    row_of = (lane192 // 32).astype(F32) * 16.0 + position + jnp.where(position > 15.5, 80.0, 0.0)
    moved = hot(i_sub.astype(F32) == row_of)
    j_column = jnp.sum(moved * j_row, axis=1, keepdims=True)
    fast_column = jnp.sum(moved * flags, axis=1, keepdims=True)
    ordered = nn(moved.astype(B16), slots).astype(B16)

    sent_hi, sent_lo = two(SF[...])
    out3 = nt(ordered, sent_hi) + nt(ordered, sent_lo)
    out3 = out3 + jnp.where(lax.broadcasted_iota(jnp.int32, (192, 256), 1) == 216, j_column, 0.0)
    for half in range(2):
        for d in range(6):
            r = half * 96 + d * 16
            send3[half, d] = out3[r : r + 16, :]
    send_constant = out3[0:96, :] * (1.0 - fast_column[0:96, :])

    pl.semaphore_wait(barrier, peers)
    start_all(STEPS - 1)

    AF[...] = jnp.zeros(AF.shape, F32)
    for d in range(3):
        AF[d * NM : (d + 1) * NM, 0:NM] = jnp.transpose(ds_ref[d])
    A3[...] = left3(AF[:, 0:64])
    for d in range(3):
        AF[d * NM : (d + 1) * NM, 0:NM] = jnp.transpose(vs_ref[d])
    V3[...] = left3(AF[:, 0:64])
    PT3[...] = left3(jnp.transpose(pf)[0:64, :])

    before = hot(iota((LN, LN), 0) < iota((LN, LN), 1)).astype(B16)
    rank = nn(jnp.broadcast_to(fast, (16, LN)).astype(B16), before)[0:1, :]
    sub = iota((LN, LN), 0)
    cm2 = jnp.concatenate([hot(sub == rank) * fast, hot(sub == rank + 64.0) * fast], axis=1).astype(B16)

    def compact_mats(ref, lead, out):
        CE[...] = jnp.zeros(CE.shape, F32)
        CO[...] = jnp.zeros(CO.shape, F32)
        for d in range(lead):
            for g in range(NF):
                r = (d * NF + g) * 8
                CE[r : r + 5, :] = ref[d, g, 0:5, :]
                CO[r : r + 4, :] = ref[d, g, 5:9, :]
        if lead == 3:
            for g in range(NF):
                CO[g * 8 + 4 : g * 8 + 5, :] = ref[1, g, 4:5, :]
        n = lead * NF * 8
        out[...] = pick(jnp.concatenate([CE[0:n, :], CO[0:n, :]], axis=1), cm2)

    compact_mats(star_ref, 3, STARF)
    compact_mats(fl_ref, 4, FLF)
    compact_mats(fa_ref, 4, FAF)

    def second(k):
        return k + 5 if k < 4 else 4

    for k in range(5):
        Yp[:, k * LN : (k + 1) * LN] = pick(jnp.concatenate([y_ref[k], y_ref[second(k)]], axis=1), cm2)

    partner = jnp.concatenate([pa_ref[c : c + 1, :] for c in range(4)], axis=1).astype(F32)
    local = hot(iota((512, 512), 0) == partner).astype(B16)
    local_fast = jnp.concatenate(
        [nn(cm2, local[0:256, :]), nn(cm2, local[256:512, :])], axis=0
    ).astype(B16)

    def to_fast(a):
        return jnp.concatenate([nt(a[:, 0:256], cm2), nt(a[:, 256:512], cm2)], axis=1).astype(B16)

    local_ff = to_fast(local_fast)
    local_fs = (local_fast.astype(F32) * slow512).astype(B16)
    ordered_fast = to_fast(ordered[0:96, :])

    slow_hi = (sent_hi.astype(F32) * slow512).astype(B16)[0:224, :]
    slow_lo = (sent_lo.astype(F32) * slow512).astype(B16)[0:224, :]
    constant = nn(slow_hi, local) + nn(slow_lo, local)
    for i in range(2):
        cols = slice(i * 256, (i + 1) * 256)
        SS[:, i * LN : (i + 1) * LN] = nt(sent_hi[:, cols], cm2) + nt(sent_lo[:, cols], cm2)

    def put_own(c, g, value):
        Z9[c * PB : (c + 1) * PB, g * LN : (g + 1) * LN] = value

    flux_full(fl_ref, put_own)

    def star_full(emit):
        for base in (0, 3, 6):
            acc = [None] * 3
            for d in range(3):
                for f in range(NF):
                    t = T9[d * NM : (d + 1) * NM, f * LN : (f + 1) * LN]
                    for q in range(3):
                        p = star_ref[d, base + q, f : f + 1, :] * t
                        acc[q] = p if acc[q] is None else acc[q] + p
            for q in range(3):
                emit(base + q, acc[q])

    T9[...] = nn(V3[...], X9[...])

    def put_base(g, value):
        SB[:, g * LN : (g + 1) * LN] = value

    star_full(put_base)

    arrive_all(STEPS - 1)
    first = jnp.concatenate([recv3[half, d] for half in range(2) for d in range(6)], axis=0)
    row192 = lax.broadcasted_iota(jnp.int32, (192, 1), 0)
    side = (row192 % 96) // 16
    remote = hot(partner == 512.0 + side.astype(F32) * 32.0 + first[:, 216:217]).astype(B16)
    remote_ff = to_fast(remote[0:96, :])
    remote_fs = (remote[0:96, :].astype(F32) * slow512).astype(B16)

    def turned(a):
        return two(jnp.transpose(a)[0:224, :])

    late_hi, late_lo = turned(first[96:192, :])
    constant = constant + nn(late_hi, remote[96:192, :]) + nn(late_lo, remote[96:192, :])
    for c in range(4):
        for g in range(NF):
            Z9[c * PB : (c + 1) * PB, g * LN : (g + 1) * LN] += constant[g * PB : (g + 1) * PB, c * LN : (c + 1) * LN]
    constant_fast = pick_two(constant, cm2)
    SB[...] += nn(PT3[...], stack3(Z9[...]))[0:NM, :]
    for k in range(5):
        Sp[:, k * LN : (k + 1) * LN] = pick(
            jnp.concatenate([SB[:, k * LN : (k + 1) * LN], SB[:, second(k) * LN : (second(k) + 1) * LN]], axis=1), cm2
        )
    slow128 = 1.0 - fast
    for g in range(NF):
        SB[:, g * LN : (g + 1) * LN] = SB[:, g * LN : (g + 1) * LN] * slow128

    def star_fast(emit):
        t01 = jnp.where(low_half, Tp[0:NM, 512:640], Tp[NM : 2 * NM, 512:640])
        for block in ((0, 5, 1, 6), (2, 7, 3, 8), (4,)):
            acc = [star_base(t01, g) + STARF[(18 + g) * 8 + 4 : (18 + g) * 8 + 5, :] * Tp[2 * NM : 3 * NM, 512:640] for g in block]
            for d in range(3):
                for k in range(4):
                    t = Tp[d * NM : (d + 1) * NM, k * LN : (k + 1) * LN]
                    for q, g in enumerate(block):
                        r = (d * NF + g) * 8 + k
                        acc[q] = acc[q] + STARF[r : r + 1, :] * t
            if len(block) == 1:
                emit(4, acc[0] + pltpu.roll(acc[0], 64, 1))
            else:
                for q in (0, 2):
                    emit(block[q], halves(acc[q], acc[q + 1]))

    def star_base(t01, g):
        return STARF[g * 8 + 4 : g * 8 + 5, :] * t01

    def halves(a, b):
        return jnp.where(low_half, a, b) + pltpu.roll(jnp.where(low_half, b, a), 64, 1)

    def flux_fast(ref, c):
        acc = [None] * NF
        for k in range(5):
            t = TRp[c * PB : (c + 1) * PB, k * LN : (k + 1) * LN]
            for g in range(NF):
                r = (c * NF + g) * 8 + k
                p = ref[r : r + 1, :] * t
                acc[g] = p if acc[g] is None else acc[g] + p
        return acc

    def put_x(k, value):
        Xp[:, k * LN : (k + 1) * LN] = stack3(rows64(value))

    def arrange(a, add):
        for k in range(5):
            for i in range(2):
                e = a[k * PB : (k + 1) * PB, i * LN : (i + 1) * LN]
                o = a[second(k) * PB : (second(k) + 1) * PB, i * LN : (i + 1) * LN]
                c = 2 * i
                v0 = jnp.where(low_half, e, pltpu.roll(o, 64, 1))
                v1 = jnp.where(low_half, pltpu.roll(e, 64, 1), o)
                cols = slice(k * LN, (k + 1) * LN)
                if add:
                    Zp[c * PB : (c + 1) * PB, cols] += v0
                    Zp[(c + 1) * PB : (c + 2) * PB, cols] += v1
                else:
                    Zp[c * PB : (c + 1) * PB, cols] = v0
                    Zp[(c + 1) * PB : (c + 2) * PB, cols] = v1

    def horner_fast():
        for k in range(5):
            put_x(k, FAST[TERMS - 1] * Sp[:, k * LN : (k + 1) * LN])

        def level(i, c):
            Tp[...] = nn(A3[...], Xp[...])

            def emit(k, value):
                total = value + c * Sp[:, k * LN : (k + 1) * LN]
                TOT[:, k * LN : (k + 1) * LN] = total
                put_x(k, total)

            star_fast(emit)
            return c * ((TERMS - 1 - i).astype(F32) * (1.0 / FINE))

        lax.fori_loop(0, TERMS - 1, level, jnp.float32(FAST[TERMS - 2]))
        for k in range(5):
            cols = slice(k * LN, (k + 1) * LN)
            value = Yp[:, cols] + TOT[:, cols]
            Yp[:, cols] = value
            put_x(k, value)

    def slow_source(s, hi, lo, r_hi, r_lo):
        got = nn(hi, local_fs) + nn(lo, local_fs) + nn(r_hi, remote_fs) + nn(r_lo, remote_fs)
        for c in range(4):
            for g in range(NF):
                Z9[c * PB : (c + 1) * PB, g * LN : (g + 1) * LN] = got[g * PB : (g + 1) * PB, c * LN : (c + 1) * LN]
        MF[s] = nn(PT3[...], stack3(Z9[...]))[0:NM, :]

    def fast_gather(hi, lo, r_hi, r_lo):
        return nn(hi, local_ff) + nn(lo, local_ff) + nn(r_hi, remote_ff) + nn(r_lo, remote_ff)

    hi, lo = two(SS[...])
    hi, lo = hi[0:224, :], lo[0:224, :]
    r_hi, r_lo = turned(first[0:96, :])
    arrange(fast_gather(hi, lo, r_hi, r_lo), False)
    Sp[...] += nn(PT3[...], stack3(Zp[...]))[0:NM, :]
    slow_source(STEPS - 1, hi, lo, r_hi, r_lo)
    horner_fast()

    for s in range(STEPS - 2, -1, -1):
        TRp[...] = nn(P3[...], Xp[...])
        for i in range(2):
            a0, a1 = flux_fast(FAF, 2 * i), flux_fast(FAF, 2 * i + 1)
            for g in range(NF):
                SS[g * PB : (g + 1) * PB, i * LN : (i + 1) * LN] = halves(a0[g], a1[g])
        hi, lo = two(SS[...])
        out = nt(ordered_fast, hi) + nt(ordered_fast, lo) + send_constant
        for d in range(6):
            send[s, d] = out[d * 16 : (d + 1) * 16, :]
        start_all(s)

        Tp[...] = nn(V3[...], Xp[...])

        def put_source(k, value):
            Sp[:, k * LN : (k + 1) * LN] = value

        star_fast(put_source)
        for c in range(4):
            acc = flux_fast(FLF, c)
            for k in range(5):
                value = halves(acc[k], acc[k + 5]) if k < 4 else acc[4] + pltpu.roll(acc[4], 64, 1)
                Zp[c * PB : (c + 1) * PB, k * LN : (k + 1) * LN] = value
        hi, lo = hi[0:224, :], lo[0:224, :]

        arrive_all(s)
        r_hi, r_lo = turned(jnp.concatenate([recv[s, d] for d in range(6)], axis=0))
        arrange(fast_gather(hi, lo, r_hi, r_lo) + constant_fast, True)
        Sp[...] += nn(PT3[...], stack3(Zp[...]))[0:NM, :]
        slow_source(s, hi, lo, r_hi, r_lo)
        if s > 0:
            horner_fast()

    spread = cm2
    s_hi, s_lo = two(Sp[...])
    y_hi, y_lo = two(Yp[...])
    for k in range(5):
        cols = slice(k * LN, (k + 1) * LN)
        source = nn(s_hi[:, cols], spread) + nn(s_lo[:, cols], spread)
        value = nn(y_hi[:, cols], spread) + nn(y_lo[:, cols], spread)
        for q, f in enumerate((k, k + 5) if k < 4 else (4,)):
            MF[0, :, f * LN : (f + 1) * LN] += source[:, q * LN : (q + 1) * LN]
            TOT9 = value[:, q * LN : (q + 1) * LN] + y_ref[f] * slow128
            o_ref[f] = TOT9

    def weighted(k, g):
        cols = slice(g * LN, (g + 1) * LN)
        total = WHOLE[k] * SB[:, cols]
        for s in range(STEPS):
            total = total + SLOW[s][k] * MF[s, :, cols]
        return total

    for g in range(NF):
        X9[:, g * LN : (g + 1) * LN] = stack3(rows64(weighted(TERMS - 1, g)))
    for k in range(TERMS - 2, -1, -1):
        T9[...] = nn(A3[...], X9[...])

        def emit(g, value):
            total = value + weighted(k, g)
            if k > 0:
                X9[:, g * LN : (g + 1) * LN] = stack3(rows64(total))
            else:
                o_ref[g] += total

        star_full(emit)

    for s in range(STEPS):
        sent_all(s)


def pick_two(a, cm2):
    return jnp.concatenate([pick(a[:, 0:256], cm2), pick(a[:, 256:512], cm2)], axis=1)


def body(
    final_adjoint, star_mats, deriv_stiff, volume_stiffness, face_projection,
    flux_local, flux_across, cluster, partner, send_slots,
):
    V = pltpu.VMEM
    D = pltpu.SemaphoreType.DMA
    scratch = [
        V((168, 192), B16), V((168, 192), B16), V((96, 192), B16), V((64, 288), B16), V((96, LN), F32), V((168, LN), F32),
        V((192, 1152), B16), V((192, 640), B16), V((168, 1152), F32), V((168, 640), F32), V((96, 1152), F32), V((96, 640), F32),
        V((256, 512), F32), V((256, 256), F32), V((288, LN), F32), V((288, LN), F32),
        V((216, LN), F32), V((288, LN), F32), V((288, LN), F32),
        V((NM, 640), F32), V((NM, 640), F32), V((NM, 1152), F32), V((STEPS, NM, 1152), F32),
        V((96, 1152), F32), V((96, 640), F32), V((NM, 640), F32),
        V((2, 6, 16, 256), F32), V((2, 6, 16, 256), F32),
        V((STEPS - 1, 6, 16, 256), F32), V((STEPS - 1, 6, 16, 256), F32),
        D((2, 6)), D((2, 6)), D((STEPS - 1, 6)), D((STEPS - 1, 6)),
    ]
    return pl.pallas_call(
        kernel,
        out_shape=jax.ShapeDtypeStruct(final_adjoint.shape, F32),
        in_specs=[pl.BlockSpec(memory_space=pltpu.VMEM)] * 10,
        out_specs=pl.BlockSpec(memory_space=pltpu.VMEM),
        scratch_shapes=scratch,
        compiler_params=pltpu.CompilerParams(collective_id=0, has_side_effects=True, vmem_limit_bytes=48 * 2**20),
        name="coarse_step",
    )(
        final_adjoint, star_mats, deriv_stiff, volume_stiffness, face_projection,
        flux_local, flux_across, cluster.reshape(1, LN), partner, send_slots,
    )


def solution(mesh):
    every = ("gx", "gy", "gz")
    in_specs = (
        P(None, None, every), P(None, None, None, every), P(), P(), P(),
        P(None, None, None, every), P(None, None, None, every), P(every), P(None, every), P(None, every),
    )
    return jax.shard_map(body, mesh=mesh, in_specs=in_specs, out_specs=P(None, None, every), check_vma=False)
```

profile of v0, /device:TPU:58, one launch (start us, length us, event | category | flops | bytes accessed | tf_op | source)
XLA Modules:
  0.0 60.4 jit_solution(17405331001828796528)
XLA Ops:
  0.0 0.8 %copy.12.fp_ref = f32[4,21,56]{2,1,0:T(8,128)S(1)} copy(f32[4,21,56]{2,0,1:T(4,128)} %param.14) | data formatting | bytes 37632 | tf_op args[4]
  0.8 0.0 copy-start.6
  0.8 1.0 %copy.11.star_ref = f32[3,9,9,128]{3,2,1,0:T(8,128)S(1)} copy(f32[3,9,9,128]{3,0,2,1:T(4,128)} %param.11) | data formatting | bytes 248832 | tf_op args[1]
  1.8 0.0 copy-done.6
  1.8 0.0 copy-start.7
  1.8 0.9 %copy-done.7 = f32[4,9,9,128]{3,0,2,1:T(4,128)S(1)} copy-done((f32[4,9,9,128]{3,0,2,1:T(4,128)S(1)}, f32[4,9,9,128]{3,0,2,1:T(4,128)}, u32[]{:S(2)}) %copy-start.7) | copy-done | bytes 165912
  2.7 0.0 copy-start
  2.7 0.0 copy-start.1
  2.7 0.0 copy-start.2
  2.7 0.0 copy-start.3
  2.7 0.0 copy-start.4
  2.7 0.0 copy-start.5
  2.8 0.9 %copy-done = f32[9,56,128]{2,1,0:T(8,128)S(1)} copy-done((f32[9,56,128]{2,1,0:T(8,128)S(1)}, f32[9,56,128]{2,1,0:T(8,128)}, u32[]{:S(2)}) %copy-start) | copy-done | bytes 258072
  3.6 0.1 copy-done.1
  3.7 0.0 copy-done.2
  3.8 0.0 copy-done.3
  3.8 0.0 copy-done.4
  3.8 0.0 copy-done.5
  3.8 56.0 %coarse_step.1 = f32[9,56,128]{2,1,0:T(8,128)S(1)} custom-call(f32[9,56,128]{2,1,0:T(8,128)S(1)} %copy-done, f32[3,9,9,128]{3,2,1,0:T(8,128)S(1)} %copy.11.star_ref, f32[3,56,56]{2,1,0:T(8,128)S(1)} %copy-done.1, f32[3,56,56]{2,1,0:T(8,128)S(1)} %copy-done.2, f32[4,21,56]{2,1,0:T(8,128)S(1)} %copy.12.fp_ref, f32[4,9,9,128]{3,2,1,0:T(8,128)S(1)} %copy.13.fl_ref, ...), custom_call_target="tpu_custom_call" | custom-call | tf_op jit(solution)/shard_map/coarse_step/pallas_call | solution.py:493
  59.7 0.7 %copy.16 = f32[9,56,128]{2,1,0:T(8,128)} copy(f32[9,56,128]{2,1,0:T(8,128)S(1)} %coarse_step.1) | data formatting | bytes 516096
  (2 shorter events, 0.1 us)
Async XLA Ops:
  0.8 1.0 %copy-start.6 = (f32[4,9,9,128]{3,0,2,1:T(4,128)S(1)}, f32[4,9,9,128]{3,0,2,1:T(4,128)}, u32[]{:S(2)}) copy-start(f32[4,9,9,128]{3,0,2,1:T(4,128)} %param.15) | copy-start | bytes 497668
  1.8 0.9 %copy-start.7 = (f32[4,9,9,128]{3,0,2,1:T(4,128)S(1)}, f32[4,9,9,128]{3,0,2,1:T(4,128)}, u32[]{:S(2)}) copy-start(f32[4,9,9,128]{3,0,2,1:T(4,128)} %param.16) | copy-start | bytes 497668
  2.7 0.9 %copy-start = (f32[9,56,128]{2,1,0:T(8,128)S(1)}, f32[9,56,128]{2,1,0:T(8,128)}, u32[]{:S(2)}) copy-start(f32[9,56,128]{2,1,0:T(8,128)} %y_ref.1) | copy-start | bytes 774148
  2.7 1.0 %copy-start.1 = (f32[3,56,56]{2,1,0:T(8,128)S(1)}, f32[3,56,56]{2,1,0:T(8,128)}, u32[]{:S(2)}) copy-start(f32[3,56,56]{2,1,0:T(8,128)} %ds_ref.1) | copy-start | bytes 112900
  2.7 1.1 %copy-start.2 = (f32[3,56,56]{2,1,0:T(8,128)S(1)}, f32[3,56,56]{2,1,0:T(8,128)}, u32[]{:S(2)}) copy-start(f32[3,56,56]{2,1,0:T(8,128)} %vs_ref.1) | copy-start | bytes 112900
  2.7 1.1 %copy-start.3 = (s32[6,32]{1,0:T(8,128)S(1)}, s32[6,32]{1,0:T(8,128)}, u32[]{:S(2)}) copy-start(s32[6,32]{1,0:T(8,128)} %ss_ref.1) | copy-start | bytes 2308
  2.7 1.1 %copy-start.4 = (s32[4,128]{1,0:T(4,128)S(1)}, s32[4,128]{1,0:T(4,128)}, u32[]{:S(2)}) copy-start(s32[4,128]{1,0:T(4,128)} %pa_ref.1) | copy-start | bytes 6148
  2.7 1.0 %copy-start.5 = (s32[128]{0:T(128)S(1)}, s32[128]{0:T(128)}, u32[]{:S(2)}) copy-start(s32[128]{0:T(128)} %param.17) | copy-start | bytes 1540
where the time goes:
time: 60.7 us; the launch traced here: 60.4 us
  Pallas kernels  56 us (92%)
  local copies, waits for them, and re-layouts  4.42 us (7%)
    pallas_call x1, Pallas kernels, body(): pl.pallas_call(kernel, out_shape=jax.ShapeDtypeStruct(final_adjoint.shape...  56 us
    unnamed x21, local copies, waits for them, and re-layouts  4.42 us

commit v1 on v0

--- a/solution.py
+++ b/solution.py
@@ -70,10 +70,20 @@
 
 
 def kernel(
-    y_ref, star_ref, ds_ref, vs_ref, fp_ref, fl_ref, fa_ref, cl_ref, pa_ref, ss_ref, o_ref,
+    y_in, star_in, ds_in, vs_in, fp_in, fl_in, fa_in, cl_in, pa_in, ss_in, o_ref,
+    y_ref, star_ref, ds_ref, vs_ref, fp_ref, fl_ref, fa_ref, cl_ref, pa_ref, ss_ref, insem,
     A3, V3, P3, PT3, PF, AF, X9, Xp, T9, Tp, TR9, TRp, SF, SS, CE, CO, STARF, FLF, FAF, Yp, Sp, SB, MF, Z9, Zp, TOT,
     send3, recv3, send, recv, ssem3, rsem3, ssem, rsem,
 ):
+    loads = [
+        pltpu.make_async_copy(a, b, insem.at[i])
+        for i, (a, b) in enumerate((
+            (fp_in, fp_ref), (y_in, y_ref), (fa_in, fa_ref), (cl_in, cl_ref), (ss_in, ss_ref),
+            (ds_in, ds_ref), (vs_in, vs_ref), (pa_in, pa_ref), (star_in, star_ref), (fl_in, fl_ref),
+        ))
+    ]
+    for load in loads:
+        load.start()
     place = [lax.axis_index(a) for a in ("gx", "gy", "gz")]
     sizes = [lax.axis_size(a) for a in ("gx", "gy", "gz")]
     sides = []
@@ -105,14 +115,14 @@
         ]
 
     def start_all(s):
-        for d in range(6):
+        for d in (5, 4, 1, 0, 3, 2):
             @pl.when(sides[d][0])
             def _():
                 for copy in link(s, d, False):
                     copy.start()
 
-    def arrive_all(s):
-        for d in range(6):
+    def arrive_all(s, which=range(6)):
+        for d in which:
             @pl.when(sides[d][0])
             def _():
                 for copy in link(s, d, True):
@@ -127,22 +137,18 @@
 
     low_half = lax.broadcasted_iota(jnp.int32, (1, LN), 1) < 64
 
-    PF[...] = jnp.zeros((96, LN), F32)
-    for c in range(4):
-        PF[c * PB : c * PB + NB, 0:NM] = fp_ref[c]
-    pf = PF[...]
-    P3[...] = left3(pf[:, 0:64])
-    SF[...] = jnp.zeros(SF.shape, F32)
-    for d in range(6):
-        there, _ = sides[d]
-
-        @pl.when(jnp.logical_not(there))
-        def _():
-            for half in range(2):
-                recv3[half, d] = jnp.zeros((16, 256), F32)
-            for s in range(STEPS - 1):
-                recv[s, d] = jnp.zeros((16, 256), F32)
-
+    for load in loads[0:5]:
+        load.wait()
+    for b in range(NB):
+        PF[b * 4 : b * 4 + 4, 0:NM] = fp_ref[b]
+    pad = jnp.zeros((PB - NB, NM), F32)
+    pf = jnp.concatenate(
+        [r for c in range(4) for r in (PF[pl.ds(c, NB, stride=4), 0:NM], pad)], axis=0
+    )
+    pf = jnp.concatenate([pf, jnp.zeros((4 * PB, 64 - NM), F32)], axis=1)
+    P3[...] = left3(pf)
+    SF[NF * PB : 256, :] = jnp.zeros((256 - NF * PB, 512), F32)
+    SS[NF * PB : 256, :] = jnp.zeros((256 - NF * PB, 256), F32)
     for f in range(NF):
         X9[:, f * LN : (f + 1) * LN] = stack3(rows64(y_ref[f]))
     TR9[...] = nn(P3[...], X9[...])
@@ -153,7 +159,7 @@
             for f in range(NF):
                 t = TR9[c * PB : (c + 1) * PB, f * LN : (f + 1) * LN]
                 for g in range(NF):
-                    p = ref[c, g, f : f + 1, :] * t
+                    p = ref[g, f, c : c + 1, :] * t
                     acc[g] = p if acc[g] is None else acc[g] + p
             for g in range(NF):
                 emit(c, g, acc[g])
@@ -200,6 +206,18 @@
     pl.semaphore_wait(barrier, peers)
     start_all(STEPS - 1)
 
+    for d in range(6):
+        there, _ = sides[d]
+
+        @pl.when(jnp.logical_not(there))
+        def _():
+            for half in range(2):
+                recv3[half, d] = jnp.zeros((16, 256), F32)
+            for s in range(STEPS - 1):
+                recv[s, d] = jnp.zeros((16, 256), F32)
+
+    for load in loads[5:]:
+        load.wait()
     AF[...] = jnp.zeros(AF.shape, F32)
     for d in range(3):
         AF[d * NM : (d + 1) * NM, 0:NM] = jnp.transpose(ds_ref[d])
@@ -207,7 +225,7 @@
     for d in range(3):
         AF[d * NM : (d + 1) * NM, 0:NM] = jnp.transpose(vs_ref[d])
     V3[...] = left3(AF[:, 0:64])
-    PT3[...] = left3(jnp.transpose(pf)[0:64, :])
+    PT3[...] = left3(jnp.transpose(pf))
 
     before = hot(iota((LN, LN), 0) < iota((LN, LN), 1)).astype(B16)
     rank = nn(jnp.broadcast_to(fast, (16, LN)).astype(B16), before)[0:1, :]
@@ -217,16 +235,15 @@
     def compact_mats(ref, lead, out):
         CE[...] = jnp.zeros(CE.shape, F32)
         CO[...] = jnp.zeros(CO.shape, F32)
-        for d in range(lead):
-            for g in range(NF):
-                r = (d * NF + g) * 8
-                CE[r : r + 5, :] = ref[d, g, 0:5, :]
-                CO[r : r + 4, :] = ref[d, g, 5:9, :]
-        if lead == 3:
-            for g in range(NF):
-                CO[g * 8 + 4 : g * 8 + 5, :] = ref[1, g, 4:5, :]
-        n = lead * NF * 8
-        out[...] = pick(jnp.concatenate([CE[0:n, :], CO[0:n, :]], axis=1), cm2)
+        for g in range(NF):
+            for k in range(5):
+                r = (g * 5 + k) * 4
+                CE[r : r + lead, :] = ref[g, k]
+                if k < 4:
+                    CO[r : r + lead, :] = ref[g, k + 5]
+                elif lead == 3:
+                    CO[r : r + 1, :] = ref[g, 4, 1:2, :]
+        out[...] = pick(jnp.concatenate([CE[...], CO[...]], axis=1), cm2)
 
     compact_mats(star_ref, 3, STARF)
     compact_mats(fl_ref, 4, FLF)
@@ -270,7 +287,7 @@
                 for f in range(NF):
                     t = T9[d * NM : (d + 1) * NM, f * LN : (f + 1) * LN]
                     for q in range(3):
-                        p = star_ref[d, base + q, f : f + 1, :] * t
+                        p = star_ref[base + q, f, d : d + 1, :] * t
                         acc[q] = p if acc[q] is None else acc[q] + p
             for q in range(3):
                 emit(base + q, acc[q])
@@ -308,25 +325,31 @@
     for g in range(NF):
         SB[:, g * LN : (g + 1) * LN] = SB[:, g * LN : (g + 1) * LN] * slow128
 
-    def star_fast(emit):
-        t01 = jnp.where(low_half, Tp[0:NM, 512:640], Tp[NM : 2 * NM, 512:640])
+    def star_fast(T, emit):
         for block in ((0, 5, 1, 6), (2, 7, 3, 8), (4,)):
-            acc = [star_base(t01, g) + STARF[(18 + g) * 8 + 4 : (18 + g) * 8 + 5, :] * Tp[2 * NM : 3 * NM, 512:640] for g in block]
-            for d in range(3):
-                for k in range(4):
-                    t = Tp[d * NM : (d + 1) * NM, k * LN : (k + 1) * LN]
+            acc = [None] * len(block)
+
+            def add(q, row, t):
+                p = STARF[row : row + 1, :] * t
+                acc[q] = p if acc[q] is None else acc[q] + p
+
+            for k in range(4):
+                for d in range(3):
+                    t = T[d * NM : (d + 1) * NM, k * LN : (k + 1) * LN]
                     for q, g in enumerate(block):
-                        r = (d * NF + g) * 8 + k
-                        acc[q] = acc[q] + STARF[r : r + 1, :] * t
+                        add(q, (g * 5 + k) * 4 + d, t)
+            last = slice(4 * LN, 5 * LN)
+            t01 = jnp.where(low_half, T[0:NM, last], T[NM : 2 * NM, last])
+            t2 = T[2 * NM : 3 * NM, last]
+            for q, g in enumerate(block):
+                add(q, (g * 5 + 4) * 4, t01)
+                add(q, (g * 5 + 4) * 4 + 2, t2)
             if len(block) == 1:
                 emit(4, acc[0] + pltpu.roll(acc[0], 64, 1))
             else:
                 for q in (0, 2):
                     emit(block[q], halves(acc[q], acc[q + 1]))
 
-    def star_base(t01, g):
-        return STARF[g * 8 + 4 : g * 8 + 5, :] * t01
-
     def halves(a, b):
         return jnp.where(low_half, a, b) + pltpu.roll(jnp.where(low_half, b, a), 64, 1)
 
@@ -335,7 +358,7 @@
         for k in range(5):
             t = TRp[c * PB : (c + 1) * PB, k * LN : (k + 1) * LN]
             for g in range(NF):
-                r = (c * NF + g) * 8 + k
+                r = (g * 5 + k) * 4 + c
                 p = ref[r : r + 1, :] * t
                 acc[g] = p if acc[g] is None else acc[g] + p
         return acc
@@ -371,7 +394,7 @@
                 TOT[:, k * LN : (k + 1) * LN] = total
                 put_x(k, total)
 
-            star_fast(emit)
+            star_fast(Tp, emit)
             return c * ((TERMS - 1 - i).astype(F32) * (1.0 / FINE))
 
         lax.fori_loop(0, TERMS - 1, level, jnp.float32(FAST[TERMS - 2]))
@@ -381,23 +404,32 @@
             Yp[:, cols] = value
             put_x(k, value)
 
-    def slow_source(s, hi, lo, r_hi, r_lo):
-        got = nn(hi, local_fs) + nn(lo, local_fs) + nn(r_hi, remote_fs) + nn(r_lo, remote_fs)
+    def gather(pairs):
+        total = None
+        for high, low, ones in pairs:
+            got = nn(high, ones) + nn(low, ones)
+            total = got if total is None else total + got
+        return total
+
+    def slow_source(s, got):
         for c in range(4):
             for g in range(NF):
                 Z9[c * PB : (c + 1) * PB, g * LN : (g + 1) * LN] = got[g * PB : (g + 1) * PB, c * LN : (c + 1) * LN]
         MF[s] = nn(PT3[...], stack3(Z9[...]))[0:NM, :]
 
-    def fast_gather(hi, lo, r_hi, r_lo):
-        return nn(hi, local_ff) + nn(lo, local_ff) + nn(r_hi, remote_ff) + nn(r_lo, remote_ff)
+    def twice(pair):
+        return jnp.concatenate(pair, axis=1)
+
+    near_ff, far_ff = remote_ff[0:64, :], jnp.concatenate([remote_ff[64:96, :]] * 2, axis=0)
+    near_fs, far_fs = remote_fs[0:64, :], jnp.concatenate([remote_fs[64:96, :]] * 2, axis=0)
 
     hi, lo = two(SS[...])
     hi, lo = hi[0:224, :], lo[0:224, :]
     r_hi, r_lo = turned(first[0:96, :])
-    arrange(fast_gather(hi, lo, r_hi, r_lo), False)
+    arrange(gather([(hi, lo, local_ff), (r_hi, r_lo, remote_ff)]), False)
     Sp[...] += nn(PT3[...], stack3(Zp[...]))[0:NM, :]
-    slow_source(STEPS - 1, hi, lo, r_hi, r_lo)
     horner_fast()
+    waiting = [(hi, lo, local_fs), (r_hi, r_lo, remote_fs)]
 
     for s in range(STEPS - 2, -1, -1):
         TRp[...] = nn(P3[...], Xp[...])
@@ -411,26 +443,41 @@
             send[s, d] = out[d * 16 : (d + 1) * 16, :]
         start_all(s)
 
+        hi, lo = hi[0:224, :], lo[0:224, :]
         Tp[...] = nn(V3[...], Xp[...])
 
         def put_source(k, value):
             Sp[:, k * LN : (k + 1) * LN] = value
 
-        star_fast(put_source)
+        star_fast(Tp, put_source)
         for c in range(4):
             acc = flux_fast(FLF, c)
             for k in range(5):
                 value = halves(acc[k], acc[k + 5]) if k < 4 else acc[4] + pltpu.roll(acc[4], 64, 1)
                 Zp[c * PB : (c + 1) * PB, k * LN : (k + 1) * LN] = value
-        hi, lo = hi[0:224, :], lo[0:224, :]
-
-        arrive_all(s)
-        r_hi, r_lo = turned(jnp.concatenate([recv[s, d] for d in range(6)], axis=0))
-        arrange(fast_gather(hi, lo, r_hi, r_lo) + constant_fast, True)
+        slow_source(s + 1, gather(waiting))
+
+        arrive_all(s, (0, 1, 2, 3))
+        r_hi, r_lo = turned(jnp.concatenate([recv[s, d] for d in range(4)], axis=0))
+        arrange(gather([(hi, lo, local_ff), (r_hi, r_lo, near_ff)]) + constant_fast, True)
         Sp[...] += nn(PT3[...], stack3(Zp[...]))[0:NM, :]
-        slow_source(s, hi, lo, r_hi, r_lo)
+        waiting = [(hi, lo, local_fs), (r_hi, r_lo, near_fs)]
+        if s == 0:
+            slow_source(0, gather(waiting))
+
+        arrive_all(s, (4, 5))
+        far = twice(turned(jnp.concatenate([recv[s, d] for d in (4, 5)], axis=0)))
+        arrange(nn(far, far_ff), False)
+        Sp[...] += nn(PT3[...], stack3(Zp[...]))[0:NM, :]
         if s > 0:
             horner_fast()
+            waiting.append((far[:, 0:32], far[:, 32:64], remote_fs[64:96, :]))
+        else:
+            got = nn(far, far_fs)
+            for c in range(4):
+                for g in range(NF):
+                    Z9[c * PB : (c + 1) * PB, g * LN : (g + 1) * LN] = got[g * PB : (g + 1) * PB, c * LN : (c + 1) * LN]
+            MF[0] += nn(PT3[...], stack3(Z9[...]))[0:NM, :]
 
     spread = cm2
     s_hi, s_lo = two(Sp[...])
@@ -479,11 +526,17 @@
 ):
     V = pltpu.VMEM
     D = pltpu.SemaphoreType.DMA
-    scratch = [
+    views = (
+        final_adjoint, jnp.transpose(star_mats, (1, 2, 0, 3)), deriv_stiff, volume_stiffness,
+        jnp.transpose(face_projection, (1, 0, 2)), jnp.transpose(flux_local, (1, 2, 0, 3)),
+        jnp.transpose(flux_across, (1, 2, 0, 3)), cluster.reshape(1, LN), partner, send_slots,
+    )
+    scratch = [V(a.shape, a.dtype) for a in views] + [
+        D((10,)),
         V((168, 192), B16), V((168, 192), B16), V((96, 192), B16), V((64, 288), B16), V((96, LN), F32), V((168, LN), F32),
         V((192, 1152), B16), V((192, 640), B16), V((168, 1152), F32), V((168, 640), F32), V((96, 1152), F32), V((96, 640), F32),
-        V((256, 512), F32), V((256, 256), F32), V((288, LN), F32), V((288, LN), F32),
-        V((216, LN), F32), V((288, LN), F32), V((288, LN), F32),
+        V((256, 512), F32), V((256, 256), F32), V((184, LN), F32), V((184, LN), F32),
+        V((184, LN), F32), V((184, LN), F32), V((184, LN), F32),
         V((NM, 640), F32), V((NM, 640), F32), V((NM, 1152), F32), V((STEPS, NM, 1152), F32),
         V((96, 1152), F32), V((96, 640), F32), V((NM, 640), F32),
         V((2, 6, 16, 256), F32), V((2, 6, 16, 256), F32),
@@ -493,15 +546,12 @@
     return pl.pallas_call(
         kernel,
         out_shape=jax.ShapeDtypeStruct(final_adjoint.shape, F32),
-        in_specs=[pl.BlockSpec(memory_space=pltpu.VMEM)] * 10,
+        in_specs=[pl.BlockSpec(memory_space=pltpu.HBM)] * 10,
         out_specs=pl.BlockSpec(memory_space=pltpu.VMEM),
         scratch_shapes=scratch,
-        compiler_params=pltpu.CompilerParams(collective_id=0, has_side_effects=True, vmem_limit_bytes=48 * 2**20),
+        compiler_params=pltpu.CompilerParams(collective_id=0, has_side_effects=True, vmem_limit_bytes=64 * 2**20),
         name="coarse_step",
-    )(
-        final_adjoint, star_mats, deriv_stiff, volume_stiffness, face_projection,
-        flux_local, flux_across, cluster.reshape(1, LN), partner, send_slots,
-    )
+    )(*views)
 
 
 def solution(mesh):

time: 60.7 us -> 55.7 us (0.918)
  the two profiles are of different devices: /device:TPU:58 before, /device:TPU:1 now
where the time goes in v1:
time: 55.7 us; the launch traced here: 55.5 us
  Pallas kernels  53.8 us (97%)
  local copies, waits for them, and re-layouts  1.66 us (3%)
    pallas_call x1, Pallas kernels, body(): pl.pallas_call(kernel, out_shape=jax.ShapeDtypeStruct(final_adjoint.shape...  53.8 us
    unnamed x1, local copies, waits for them, and re-layouts  1.66 us

profile of v1, /device:TPU:1, one launch (start us, length us, event | category | flops | bytes accessed | tf_op | source)
XLA Modules:
  0.0 55.5 jit_solution(7995405158074951464)
XLA Ops:
  0.0 53.8 %coarse_step.1 = f32[9,56,128]{2,1,0:T(8,128)} custom-call(f32[9,56,128]{2,1,0:T(8,128)} %y_in.1, f32[9,9,3,128]{3,2,1,0:T(4,128)} %bitcast.5, f32[3,56,56]{2,1,0:T(8,128)} %ds_in.1, f32[3,56,56]{2,1,0:T(8,128)} %vs_in.1, f32[21,4,56]{2,1,0:T(4,128)} %bitcast.8, f32[9,9,4,128]{3,2,1,0:T(4,128)} %bitcast.6, f32[9,9,4,128]{3,2,1,0:T(4,128)} %bitcast.7, ...), custom_call_target="tpu_custom_call" | custom-call | tf_op jit(solution)/shard_map/coarse_step/pallas_call | solution.py:546
  53.8 1.7 %copy.12 = f32[9,56,128]{2,1,0:T(8,128)} copy(f32[9,56,128]{2,1,0:T(8,128)} %coarse_step.1) | data formatting | bytes 516096

commit v2 on v1

--- a/solution.py
+++ b/solution.py
@@ -72,7 +72,7 @@
 def kernel(
     y_in, star_in, ds_in, vs_in, fp_in, fl_in, fa_in, cl_in, pa_in, ss_in, o_ref,
     y_ref, star_ref, ds_ref, vs_ref, fp_ref, fl_ref, fa_ref, cl_ref, pa_ref, ss_ref, insem,
-    A3, V3, P3, PT3, PF, AF, X9, Xp, T9, Tp, TR9, TRp, SF, SS, CE, CO, STARF, FLF, FAF, Yp, Sp, SB, MF, Z9, Zp, TOT,
+    A3, V3, P3, PT3, PF, AF, X9, Xp, T9, Tp, TR9, TRp, SF, SS, CE, CO, STARF, FLF, FAF, Yp, Sp, SB, MF, Z9, Zp, Tq, U9, WK,
     send3, recv3, send, recv, ssem3, rsem3, ssem, rsem,
 ):
     loads = [
@@ -280,42 +280,36 @@
 
     flux_full(fl_ref, put_own)
 
-    def star_full(emit):
+    def star_full(T, emit):
         for base in (0, 3, 6):
             acc = [None] * 3
-            for d in range(3):
-                for f in range(NF):
-                    t = T9[d * NM : (d + 1) * NM, f * LN : (f + 1) * LN]
+            for f in range(NF):
+                for d in range(3):
+                    t = T[d * NM : (d + 1) * NM, f * LN : (f + 1) * LN]
                     for q in range(3):
                         p = star_ref[base + q, f, d : d + 1, :] * t
                         acc[q] = p if acc[q] is None else acc[q] + p
-            for q in range(3):
-                emit(base + q, acc[q])
+            emit(base, acc)
 
     T9[...] = nn(V3[...], X9[...])
 
-    def put_base(g, value):
-        SB[:, g * LN : (g + 1) * LN] = value
-
-    star_full(put_base)
-
-    arrive_all(STEPS - 1)
-    first = jnp.concatenate([recv3[half, d] for half in range(2) for d in range(6)], axis=0)
-    row192 = lax.broadcasted_iota(jnp.int32, (192, 1), 0)
-    side = (row192 % 96) // 16
-    remote = hot(partner == 512.0 + side.astype(F32) * 32.0 + first[:, 216:217]).astype(B16)
-    remote_ff = to_fast(remote[0:96, :])
-    remote_fs = (remote[0:96, :].astype(F32) * slow512).astype(B16)
-
-    def turned(a):
-        return two(jnp.transpose(a)[0:224, :])
-
-    late_hi, late_lo = turned(first[96:192, :])
-    constant = constant + nn(late_hi, remote[96:192, :]) + nn(late_lo, remote[96:192, :])
-    for c in range(4):
-        for g in range(NF):
-            Z9[c * PB : (c + 1) * PB, g * LN : (g + 1) * LN] += constant[g * PB : (g + 1) * PB, c * LN : (c + 1) * LN]
-    constant_fast = pick_two(constant, cm2)
+    def put_base(base, values):
+        for q in range(3):
+            SB[:, (base + q) * LN : (base + q + 1) * LN] = values[q]
+
+    star_full(T9, put_base)
+
+    def place_all(got, add):
+        for c in range(4):
+            for g in range(NF):
+                value = got[g * PB : (g + 1) * PB, c * LN : (c + 1) * LN]
+                at = (slice(c * PB, (c + 1) * PB), slice(g * LN, (g + 1) * LN))
+                if add:
+                    Z9[at] += value
+                else:
+                    Z9[at] = value
+
+    place_all(constant, True)
     SB[...] += nn(PT3[...], stack3(Z9[...]))[0:NM, :]
     for k in range(5):
         Sp[:, k * LN : (k + 1) * LN] = pick(
@@ -324,6 +318,18 @@
     slow128 = 1.0 - fast
     for g in range(NF):
         SB[:, g * LN : (g + 1) * LN] = SB[:, g * LN : (g + 1) * LN] * slow128
+
+    def turned(a):
+        return two(jnp.transpose(a)[0:224, :])
+
+    def remote_slots(rows, dirs):
+        n = len(dirs) * 16
+        row = lax.broadcasted_iota(jnp.int32, (2 * n, 1), 0)
+        side = ((row % n) // 16 + dirs[0]).astype(F32)
+        return hot(partner == 512.0 + side * 32.0 + rows[:, 216:217]).astype(B16)
+
+    def masked(a):
+        return (a.astype(F32) * slow512).astype(B16)
 
     def star_fast(T, emit):
         for block in ((0, 5, 1, 6), (2, 7, 3, 8), (4,)):
@@ -382,27 +388,41 @@
                     Zp[c * PB : (c + 1) * PB, cols] = v0
                     Zp[(c + 1) * PB : (c + 2) * PB, cols] = v1
 
+    def multiply(T, first, values):
+        x = jnp.concatenate([stack3(rows64(v)) for v in values], axis=1)
+        T[:, first * LN : (first + len(values)) * LN] = nn(A3[...], x)
+
+    def fast_level(T, c, out):
+        held = []
+
+        def emit(k, value):
+            held.append(value + c * Sp[:, k * LN : (k + 1) * LN])
+            if k in (1, 3, 4):
+                multiply(out, k + 1 - len(held), held)
+                held.clear()
+
+        star_fast(T, emit)
+
     def horner_fast():
-        for k in range(5):
-            put_x(k, FAST[TERMS - 1] * Sp[:, k * LN : (k + 1) * LN])
-
-        def level(i, c):
-            Tp[...] = nn(A3[...], Xp[...])
-
-            def emit(k, value):
-                total = value + c * Sp[:, k * LN : (k + 1) * LN]
-                TOT[:, k * LN : (k + 1) * LN] = total
-                put_x(k, total)
-
-            star_fast(Tp, emit)
-            return c * ((TERMS - 1 - i).astype(F32) * (1.0 / FINE))
-
-        lax.fori_loop(0, TERMS - 1, level, jnp.float32(FAST[TERMS - 2]))
-        for k in range(5):
+        for group in ((0, 1), (2, 3), (4,)):
+            multiply(Tp, group[0], [FAST[TERMS - 1] * Sp[:, k * LN : (k + 1) * LN] for k in group])
+
+        def levels(i, c):
+            k = (TERMS - 1 - 2 * i).astype(F32)
+            fast_level(Tp, c, Tq)
+            c = c * (k * (1.0 / FINE))
+            fast_level(Tq, c, Tp)
+            return c * ((k - 1.0) * (1.0 / FINE))
+
+        lax.fori_loop(0, (TERMS - 2) // 2, levels, jnp.float32(FAST[TERMS - 2]))
+
+        def emit(k, value):
             cols = slice(k * LN, (k + 1) * LN)
-            value = Yp[:, cols] + TOT[:, cols]
+            value = Yp[:, cols] + (value + FAST[0] * Sp[:, cols])
             Yp[:, cols] = value
             put_x(k, value)
+
+        star_fast(Tp, emit)
 
     def gather(pairs):
         total = None
@@ -412,24 +432,34 @@
         return total
 
     def slow_source(s, got):
-        for c in range(4):
-            for g in range(NF):
-                Z9[c * PB : (c + 1) * PB, g * LN : (g + 1) * LN] = got[g * PB : (g + 1) * PB, c * LN : (c + 1) * LN]
+        place_all(got, False)
         MF[s] = nn(PT3[...], stack3(Z9[...]))[0:NM, :]
 
     def twice(pair):
         return jnp.concatenate(pair, axis=1)
 
-    near_ff, far_ff = remote_ff[0:64, :], jnp.concatenate([remote_ff[64:96, :]] * 2, axis=0)
-    near_fs, far_fs = remote_fs[0:64, :], jnp.concatenate([remote_fs[64:96, :]] * 2, axis=0)
-
     hi, lo = two(SS[...])
     hi, lo = hi[0:224, :], lo[0:224, :]
-    r_hi, r_lo = turned(first[0:96, :])
-    arrange(gather([(hi, lo, local_ff), (r_hi, r_lo, remote_ff)]), False)
-    Sp[...] += nn(PT3[...], stack3(Zp[...]))[0:NM, :]
+    local_part = gather([(hi, lo, local_ff)])
+    arrange(local_part, False)
+    waiting = [(hi, lo, local_fs)]
+    late = []
+    later = []
+    for dirs in ((0, 1, 2, 3), (4, 5)):
+        n = 16 * len(dirs)
+        arrive_all(STEPS - 1, dirs)
+        rows = jnp.concatenate([recv3[half, d] for half in range(2) for d in dirs], axis=0)
+        remote = remote_slots(rows, dirs)
+        remote_ff = to_fast(remote)
+        r_hi, r_lo = turned(rows)
+        arrange(gather([(r_hi, r_lo, remote_ff)]), dirs[0] == 0)
+        Sp[...] += nn(PT3[...], stack3(Zp[...]))[0:NM, :]
+        late.append((rows, remote, n))
+        later.append((remote_ff[0:n, :], remote))
     horner_fast()
-    waiting = [(hi, lo, local_fs), (r_hi, r_lo, remote_fs)]
+    near_ff = later[0][0]
+    far_ff = jnp.concatenate([later[1][0]] * 2, axis=0)
+    far_all = jnp.concatenate([later[1][1][0:32, :]] * 2, axis=0)
 
     for s in range(STEPS - 2, -1, -1):
         TRp[...] = nn(P3[...], Xp[...])
@@ -455,6 +485,18 @@
             for k in range(5):
                 value = halves(acc[k], acc[k + 5]) if k < 4 else acc[4] + pltpu.roll(acc[4], 64, 1)
                 Zp[c * PB : (c + 1) * PB, k * LN : (k + 1) * LN] = value
+        if s == STEPS - 2:
+            terms = []
+            for rows, remote, n in late:
+                r_hi, r_lo = turned(rows[0:n, :])
+                waiting.append((r_hi, r_lo, masked(remote[0:n, :])))
+                r_hi, r_lo = turned(rows[n : 2 * n, :])
+                terms.append((r_hi, r_lo, remote[n : 2 * n, :]))
+            extra = gather(terms)
+            constant_fast = pick_two(constant + extra, cm2)
+            place_all(extra * slow512, False)
+            SB[...] += nn(PT3[...], stack3(Z9[...]))[0:NM, :]
+            near_fs, far_fs = masked(late[0][1][0:64, :]), masked(late[1][1][0:32, :])
         slow_source(s + 1, gather(waiting))
 
         arrive_all(s, (0, 1, 2, 3))
@@ -464,53 +506,52 @@
         waiting = [(hi, lo, local_fs), (r_hi, r_lo, near_fs)]
         if s == 0:
             slow_source(0, gather(waiting))
+            s_hi, s_lo = two(Sp[...])
+            y_hi, y_lo = two(Yp[...])
+            for k in range(5):
+                cols = slice(k * LN, (k + 1) * LN)
+                source = nn(s_hi[:, cols], cm2) + nn(s_lo[:, cols], cm2)
+                value = nn(y_hi[:, cols], cm2) + nn(y_lo[:, cols], cm2)
+                for q, f in enumerate((k, k + 5) if k < 4 else (4,)):
+                    MF[0, :, f * LN : (f + 1) * LN] += source[:, q * LN : (q + 1) * LN]
+                    o_ref[f] = value[:, q * LN : (q + 1) * LN] + y_ref[f] * slow128
+            for g in range(NF):
+                cols = slice(g * LN, (g + 1) * LN)
+                base, parts = SB[:, cols], [MF[q, :, cols] for q in range(STEPS)]
+                for k in range(TERMS):
+                    total = WHOLE[k] * base
+                    for q in range(STEPS):
+                        total = total + SLOW[q][k] * parts[q]
+                    WK[k, :, cols] = total
 
         arrive_all(s, (4, 5))
-        far = twice(turned(jnp.concatenate([recv[s, d] for d in (4, 5)], axis=0)))
-        arrange(nn(far, far_ff), False)
-        Sp[...] += nn(PT3[...], stack3(Zp[...]))[0:NM, :]
+        far = jnp.concatenate(turned(jnp.concatenate([recv[s, d] for d in (4, 5)], axis=0)), axis=1)
         if s > 0:
+            arrange(nn(far, far_ff), False)
+            Sp[...] += nn(PT3[...], stack3(Zp[...]))[0:NM, :]
             horner_fast()
-            waiting.append((far[:, 0:32], far[:, 32:64], remote_fs[64:96, :]))
+            waiting.append((far[:, 0:32], far[:, 32:64], far_fs))
         else:
-            got = nn(far, far_fs)
-            for c in range(4):
-                for g in range(NF):
-                    Z9[c * PB : (c + 1) * PB, g * LN : (g + 1) * LN] = got[g * PB : (g + 1) * PB, c * LN : (c + 1) * LN]
-            MF[0] += nn(PT3[...], stack3(Z9[...]))[0:NM, :]
-
-    spread = cm2
-    s_hi, s_lo = two(Sp[...])
-    y_hi, y_lo = two(Yp[...])
-    for k in range(5):
-        cols = slice(k * LN, (k + 1) * LN)
-        source = nn(s_hi[:, cols], spread) + nn(s_lo[:, cols], spread)
-        value = nn(y_hi[:, cols], spread) + nn(y_lo[:, cols], spread)
-        for q, f in enumerate((k, k + 5) if k < 4 else (4,)):
-            MF[0, :, f * LN : (f + 1) * LN] += source[:, q * LN : (q + 1) * LN]
-            TOT9 = value[:, q * LN : (q + 1) * LN] + y_ref[f] * slow128
-            o_ref[f] = TOT9
+            slow_source(0, nn(far, far_all))
 
     def weighted(k, g):
         cols = slice(g * LN, (g + 1) * LN)
-        total = WHOLE[k] * SB[:, cols]
-        for s in range(STEPS):
-            total = total + SLOW[s][k] * MF[s, :, cols]
-        return total
-
-    for g in range(NF):
-        X9[:, g * LN : (g + 1) * LN] = stack3(rows64(weighted(TERMS - 1, g)))
+        return WK[k, :, cols] + SLOW[0][k] * MF[0, :, cols]
+
+    for base in (0, 3, 6):
+        multiply(T9, base, [weighted(TERMS - 1, base + q) for q in range(3)])
+    here, there = T9, U9
     for k in range(TERMS - 2, -1, -1):
-        T9[...] = nn(A3[...], X9[...])
-
-        def emit(g, value):
-            total = value + weighted(k, g)
+        def emit(base, values):
+            totals = [values[q] + weighted(k, base + q) for q in range(3)]
             if k > 0:
-                X9[:, g * LN : (g + 1) * LN] = stack3(rows64(total))
+                multiply(there, base, totals)
             else:
-                o_ref[g] += total
-
-        star_full(emit)
+                for q in range(3):
+                    o_ref[base + q] += totals[q]
+
+        star_full(here, emit)
+        here, there = there, here
 
     for s in range(STEPS):
         sent_all(s)
@@ -538,7 +579,7 @@
         V((256, 512), F32), V((256, 256), F32), V((184, LN), F32), V((184, LN), F32),
         V((184, LN), F32), V((184, LN), F32), V((184, LN), F32),
         V((NM, 640), F32), V((NM, 640), F32), V((NM, 1152), F32), V((STEPS, NM, 1152), F32),
-        V((96, 1152), F32), V((96, 640), F32), V((NM, 640), F32),
+        V((96, 1152), F32), V((96, 640), F32), V((168, 640), F32), V((168, 1152), F32), V((TERMS, NM, 1152), F32),
         V((2, 6, 16, 256), F32), V((2, 6, 16, 256), F32),
         V((STEPS - 1, 6, 16, 256), F32), V((STEPS - 1, 6, 16, 256), F32),
         D((2, 6)), D((2, 6)), D((STEPS - 1, 6)), D((STEPS - 1, 6)),

time: 55.7 us -> 52.9 us (0.950)
  Pallas kernels: 53.8 us -> 51.1 us
    pallas_call x1, Pallas kernels: 53.8 us -> 51.1 us  [body(): pl.pallas_call(kernel, out_shape=jax.ShapeDtypeStruct(final_adjoint.shape...]
where the time goes in v2:
time: 52.9 us; the launch traced here: 52.8 us
  Pallas kernels  51.1 us (97%)
  local copies, waits for them, and re-layouts  1.66 us (3%)
    pallas_call x1, Pallas kernels, body(): pl.pallas_call(kernel, out_shape=jax.ShapeDtypeStruct(final_adjoint.shape...  51.1 us
    unnamed x1, local copies, waits for them, and re-layouts  1.66 us

profile of v2, /device:TPU:1, one launch (start us, length us, event | category | flops | bytes accessed | tf_op | source)
XLA Modules:
  0.0 52.8 jit_solution(3757722976524015394)
XLA Ops:
  0.0 51.1 %coarse_step.1 = f32[9,56,128]{2,1,0:T(8,128)} custom-call(f32[9,56,128]{2,1,0:T(8,128)} %y_in.1, f32[9,9,3,128]{3,2,1,0:T(4,128)} %bitcast.5, f32[3,56,56]{2,1,0:T(8,128)} %ds_in.1, f32[3,56,56]{2,1,0:T(8,128)} %vs_in.1, f32[21,4,56]{2,1,0:T(4,128)} %bitcast.8, f32[9,9,4,128]{3,2,1,0:T(4,128)} %bitcast.6, f32[9,9,4,128]{3,2,1,0:T(4,128)} %bitcast.7, ...), custom_call_target="tpu_custom_call" | custom-call | tf_op jit(solution)/shard_map/coarse_step/pallas_call | solution.py:587
  51.1 1.7 %copy.12 = f32[9,56,128]{2,1,0:T(8,128)} copy(f32[9,56,128]{2,1,0:T(8,128)} %coarse_step.1) | data formatting | bytes 516096

commit v3 on v2

--- a/solution.py
+++ b/solution.py
@@ -70,8 +70,8 @@
 
 
 def kernel(
-    y_in, star_in, ds_in, vs_in, fp_in, fl_in, fa_in, cl_in, pa_in, ss_in, o_ref,
-    y_ref, star_ref, ds_ref, vs_ref, fp_ref, fl_ref, fa_ref, cl_ref, pa_ref, ss_ref, insem,
+    y_in, star_in, ds_in, vs_in, fp_in, fl_in, fa_in, cl_in, pa_in, ss_in, o_out,
+    y_ref, star_ref, ds_ref, vs_ref, fp_ref, fl_ref, fa_ref, cl_ref, pa_ref, ss_ref, insem, o_ref, osem,
     A3, V3, P3, PT3, PF, AF, X9, Xp, T9, Tp, TR9, TRp, SF, SS, CE, CO, STARF, FLF, FAF, Yp, Sp, SB, MF, Z9, Zp, Tq, U9, WK,
     send3, recv3, send, recv, ssem3, rsem3, ssem, rsem,
 ):
@@ -82,8 +82,6 @@
             (ds_in, ds_ref), (vs_in, vs_ref), (pa_in, pa_ref), (star_in, star_ref), (fl_in, fl_ref),
         ))
     ]
-    for load in loads:
-        load.start()
     place = [lax.axis_index(a) for a in ("gx", "gy", "gz")]
     sizes = [lax.axis_size(a) for a in ("gx", "gy", "gz")]
     sides = []
@@ -96,10 +94,13 @@
     peers = sum(there.astype(jnp.int32) for there, _ in sides)
 
     barrier = pltpu.get_barrier_semaphore()
-    for there, target in sides:
+    for there, target in sides[::-1]:
         @pl.when(there)
         def _():
             pl.semaphore_signal(barrier, inc=1, device_id=target, device_id_type=MESH)
+
+    for load in loads:
+        load.start()
 
     def link(s, d, arriving):
         to = d if arriving else d ^ 1
@@ -407,20 +408,19 @@
         for group in ((0, 1), (2, 3), (4,)):
             multiply(Tp, group[0], [FAST[TERMS - 1] * Sp[:, k * LN : (k + 1) * LN] for k in group])
 
-        def levels(i, c):
-            k = (TERMS - 1 - 2 * i).astype(F32)
-            fast_level(Tp, c, Tq)
-            c = c * (k * (1.0 / FINE))
-            fast_level(Tq, c, Tp)
-            return c * ((k - 1.0) * (1.0 / FINE))
-
-        lax.fori_loop(0, (TERMS - 2) // 2, levels, jnp.float32(FAST[TERMS - 2]))
+        here, there = Tp, Tq
+        for k in range(TERMS - 2, 0, -1):
+            fast_level(here, FAST[k], there)
+            here, there = there, here
 
         def emit(k, value):
             cols = slice(k * LN, (k + 1) * LN)
             value = Yp[:, cols] + (value + FAST[0] * Sp[:, cols])
             Yp[:, cols] = value
             put_x(k, value)
+            if k in (1, 3, 4):
+                group = slice((k - k % 2 if k < 4 else 4) * LN, (k + 1) * LN)
+                TRp[:, group] = nn(P3[...], Xp[:, group])
 
         star_fast(Tp, emit)
 
@@ -458,11 +458,17 @@
         later.append((remote_ff[0:n, :], remote))
     horner_fast()
     near_ff = later[0][0]
-    far_ff = jnp.concatenate([later[1][0]] * 2, axis=0)
+    far_slots = later[1][1][0:32, :]
+    far_pairs = jnp.concatenate(
+        [
+            jnp.concatenate([nt(far_slots[:, c * LN : (c + 1) * LN], cm2[:, q * LN : (q + 1) * LN]) for c in range(4)], axis=1)
+            for q in (0, 1, 0, 1)
+        ],
+        axis=0,
+    ).astype(B16)
     far_all = jnp.concatenate([later[1][1][0:32, :]] * 2, axis=0)
 
     for s in range(STEPS - 2, -1, -1):
-        TRp[...] = nn(P3[...], Xp[...])
         for i in range(2):
             a0, a1 = flux_fast(FAF, 2 * i), flux_fast(FAF, 2 * i + 1)
             for g in range(NF):
@@ -525,14 +531,19 @@
                     WK[k, :, cols] = total
 
         arrive_all(s, (4, 5))
-        far = jnp.concatenate(turned(jnp.concatenate([recv[s, d] for d in (4, 5)], axis=0)), axis=1)
+        came = jnp.concatenate([recv[s, d] for d in (4, 5)], axis=0)
         if s > 0:
-            arrange(nn(far, far_ff), False)
+            a = jnp.transpose(came)
+            odd = jnp.concatenate([a[5 * PB : 9 * PB, :], a[4 * PB : 5 * PB, :]], axis=0)
+            paired = nn(jnp.concatenate(two(jnp.concatenate([a[0 : 5 * PB, :], odd], axis=1)), axis=1), far_pairs)
+            for c in range(4):
+                for k in range(5):
+                    Zp[c * PB : (c + 1) * PB, k * LN : (k + 1) * LN] = paired[k * PB : (k + 1) * PB, c * LN : (c + 1) * LN]
             Sp[...] += nn(PT3[...], stack3(Zp[...]))[0:NM, :]
             horner_fast()
-            waiting.append((far[:, 0:32], far[:, 32:64], far_fs))
+            waiting.append((*turned(came), far_fs))
         else:
-            slow_source(0, nn(far, far_all))
+            slow_source(0, nn(jnp.concatenate(turned(came), axis=1), far_all))
 
     def weighted(k, g):
         cols = slice(g * LN, (g + 1) * LN)
@@ -541,6 +552,9 @@
     for base in (0, 3, 6):
         multiply(T9, base, [weighted(TERMS - 1, base + q) for q in range(3)])
     here, there = T9, U9
+    stores = [
+        pltpu.make_async_copy(o_ref.at[pl.ds(3 * i, 3)], o_out.at[pl.ds(3 * i, 3)], osem.at[i]) for i in range(3)
+    ]
     for k in range(TERMS - 2, -1, -1):
         def emit(base, values):
             totals = [values[q] + weighted(k, base + q) for q in range(3)]
@@ -549,12 +563,15 @@
             else:
                 for q in range(3):
                     o_ref[base + q] += totals[q]
+                stores[base // 3].start()
 
         star_full(here, emit)
         here, there = there, here
 
     for s in range(STEPS):
         sent_all(s)
+    for store in stores:
+        store.wait()
 
 
 def pick_two(a, cm2):
@@ -573,7 +590,7 @@
         jnp.transpose(flux_across, (1, 2, 0, 3)), cluster.reshape(1, LN), partner, send_slots,
     )
     scratch = [V(a.shape, a.dtype) for a in views] + [
-        D((10,)),
+        D((10,)), V(final_adjoint.shape, F32), D((3,)),
         V((168, 192), B16), V((168, 192), B16), V((96, 192), B16), V((64, 288), B16), V((96, LN), F32), V((168, LN), F32),
         V((192, 1152), B16), V((192, 640), B16), V((168, 1152), F32), V((168, 640), F32), V((96, 1152), F32), V((96, 640), F32),
         V((256, 512), F32), V((256, 256), F32), V((184, LN), F32), V((184, LN), F32),
@@ -588,7 +605,7 @@
         kernel,
         out_shape=jax.ShapeDtypeStruct(final_adjoint.shape, F32),
         in_specs=[pl.BlockSpec(memory_space=pltpu.HBM)] * 10,
-        out_specs=pl.BlockSpec(memory_space=pltpu.VMEM),
+        out_specs=pl.BlockSpec(memory_space=pltpu.HBM),
         scratch_shapes=scratch,
         compiler_params=pltpu.CompilerParams(collective_id=0, has_side_effects=True, vmem_limit_bytes=64 * 2**20),
         name="coarse_step",

time: 52.9 us -> 52.2 us (0.987)
  Pallas kernels: 51.1 us -> 50.4 us
    pallas_call x1, Pallas kernels: 51.1 us -> 50.4 us  [body(): pl.pallas_call(kernel, out_shape=jax.ShapeDtypeStruct(final_adjoint.shape...]
where the time goes in v3:
time: 52.2 us; the launch traced here: 52 us
  Pallas kernels  50.4 us (97%)
  local copies, waits for them, and re-layouts  1.66 us (3%)
    pallas_call x1, Pallas kernels, body(): pl.pallas_call(kernel, out_shape=jax.ShapeDtypeStruct(final_adjoint.shape...  50.4 us
    unnamed x1, local copies, waits for them, and re-layouts  1.66 us

profile of v3, /device:TPU:1, one launch (start us, length us, event | category | flops | bytes accessed | tf_op | source)
XLA Modules:
  0.0 52.0 jit_solution(6700827962219909074)
XLA Ops:
  0.0 50.4 %coarse_step.1 = f32[9,56,128]{2,1,0:T(8,128)} custom-call(f32[9,56,128]{2,1,0:T(8,128)} %y_in.1, f32[9,9,3,128]{3,2,1,0:T(4,128)} %bitcast.5, f32[3,56,56]{2,1,0:T(8,128)} %ds_in.1, f32[3,56,56]{2,1,0:T(8,128)} %vs_in.1, f32[21,4,56]{2,1,0:T(4,128)} %bitcast.8, f32[9,9,4,128]{3,2,1,0:T(4,128)} %bitcast.6, f32[9,9,4,128]{3,2,1,0:T(4,128)} %bitcast.7, ...), custom_call_target="tpu_custom_call" | custom-call | tf_op jit(solution)/shard_map/coarse_step/pallas_call | solution.py:604
  50.4 1.7 %copy.12 = f32[9,56,128]{2,1,0:T(8,128)} copy(f32[9,56,128]{2,1,0:T(8,128)} %coarse_step.1) | data formatting | bytes 516096
